TPU v7x, 1024 devices: a whole 4x8x16 slice. The times are simulated.
1024 devices in a mesh: expert: 32 (over z, core), dp: 32 (over x, y).
Axes of the slice: x: 4, y: 8, z: 16, core: 2. Of those that a mesh axis runs over, the one named last changes fastest.
Arguments:
- tokens: bfloat16 [1024, 4096], P('expert', 'dp'), may hold values from -6 to 6
- grad_out: bfloat16 [1024, 4096], P('expert', 'dp'), may hold values from -3 to 3
- expert_ids: int32 [1024, 8], P('expert'), may hold values from 0 to 31, all different within a row; in each aligned block of 32 rows (0 to 31, 32 to 63, ...) at most 16 rows name the same one
- probs: bfloat16 [1024, 8], P('expert'), may hold values from 0.099609375 to 0.5
- gate_weight: bfloat16 [32, 4096, 1536], P('expert', 'dp'), may hold values from -0.09375 to 0.09375
- up_weight: bfloat16 [32, 4096, 1536], P('expert', 'dp'), may hold values from -0.09375 to 0.09375
- down_weight: bfloat16 [32, 1536, 4096], P('expert', None, 'dp'), may hold values from -0.15625 to 0.15625
Outputs:
- grad_tokens: bfloat16 [1024, 4096], P('expert', 'dp')
- grad_probs: bfloat16 [1024, 8], P('expert')
- grad_gate: float32 [32, 4096, 1536], P('expert', 'dp')
- grad_up: float32 [32, 4096, 1536], P('expert', 'dp')
- grad_down: float32 [32, 1536, 4096], P('expert', None, 'dp')
Inputs may be any that keep to these rules, and one draw needn't show every extreme that they name: `expert_ids`: each row names 8 different experts. Among the routes of the 32 tokens of one index of expert no expert is named more than 16 times, and in at least one such block some expert is named exactly 16 times.
All inputs are finite; a program needn't handle non-finite values.
Results may differ from a plain program's by a relative error of at most 0.0057.
Values may be sent and summed in bfloat16 or wider, within the bound.
A program may use at most 64 MiB of HBM per device.

v0:
```python
import jax
import jax.numpy as jnp
from jax import lax
from jax.sharding import PartitionSpec as P


def contract_last(left_side, right_side):
    return lax.dot_general(
        left_side, right_side, (((1,), (1,)), ((), ())), preferred_element_type=jnp.float32
    )


def contract_first(left_side, right_side):
    return lax.dot_general(
        left_side, right_side, (((0,), (0,)), ((), ())), preferred_element_type=jnp.float32
    )


def swiglu_backward(gate_sum, up_sum, back_sum, route_weight):
    sigmoid_gate = jax.nn.sigmoid(gate_sum)
    active = gate_sum * sigmoid_gate
    product = active * up_sum
    grad_weight = jnp.sum(back_sum * product, axis=1).astype(jnp.bfloat16)
    scaled = route_weight[:, None] * back_sum
    grad_gate_pre = (
        scaled * up_sum * sigmoid_gate * (1.0 + gate_sum * (1.0 - sigmoid_gate))
    ).astype(jnp.bfloat16)
    grad_up_pre = (scaled * active).astype(jnp.bfloat16)
    weighted = (route_weight[:, None] * product).astype(jnp.bfloat16)
    return (jnp.concatenate((weighted, grad_gate_pre, grad_up_pre), axis=1), grad_weight)


def per_device(tokens, grad_out, expert_ids, probs, gate_weight, up_weight, down_weight):
    tok_dev, features = tokens.shape
    per_token = expert_ids.shape[1]
    hidden = gate_weight.shape[2]
    experts = lax.axis_size("expert")
    routes = tok_dev * per_token
    capacity = min(tok_dev, 2 * routes // experts)
    total_rows = experts * capacity
    w_gate = gate_weight[0]
    w_up = up_weight[0]
    w_down = down_weight[0]
    flat_ids = expert_ids.reshape(routes)
    onehot = (flat_ids[:, None] == jnp.arange(experts, dtype=jnp.int32)[None, :]).astype(jnp.int32)
    earlier = jnp.cumsum(onehot, axis=0) - onehot
    slot_of = jnp.sum(earlier * onehot, axis=1)
    position = flat_ids * capacity + slot_of
    spread_x = jnp.broadcast_to(tokens[:, None, :], (tok_dev, per_token, features)).reshape(
        routes, features
    )
    spread_dy = jnp.broadcast_to(grad_out[:, None, :], (tok_dev, per_token, features)).reshape(
        routes, features
    )
    send_x = jnp.zeros((total_rows, features), jnp.bfloat16).at[position].set(spread_x)
    send_dy = jnp.zeros((total_rows, features), jnp.bfloat16).at[position].set(spread_dy)
    send_p = jnp.zeros((total_rows,), jnp.bfloat16).at[position].set(probs.reshape(routes))
    recv_x, recv_dy, recv_p = (
        lax.all_to_all(
            send_x.reshape(experts, capacity, features),
            "expert",
            split_axis=0,
            concat_axis=0,
            tiled=True,
        ),
        lax.all_to_all(
            send_dy.reshape(experts, capacity, features),
            "expert",
            split_axis=0,
            concat_axis=0,
            tiled=True,
        ),
        lax.all_to_all(
            send_p.reshape(experts, capacity), "expert", split_axis=0, concat_axis=0, tiled=True
        ),
    )
    rows_x = recv_x.reshape(total_rows, features)
    rows_dy = recv_dy.reshape(total_rows, features)
    rows_p = recv_p.reshape(total_rows).astype(jnp.float32)
    part_x = rows_x
    part_dy = rows_dy
    gate_part = jnp.dot(part_x, w_gate, preferred_element_type=jnp.float32)
    up_part = jnp.dot(part_x, w_up, preferred_element_type=jnp.float32)
    back_part = contract_last(part_dy, w_down)
    summed = lax.psum_scatter(
        jnp.concatenate((gate_part, up_part, back_part), axis=1),
        "dp",
        scatter_dimension=0,
        tiled=True,
    )
    gathered = lax.all_gather(summed, "dp", axis=0, tiled=True)
    stacked, grad_weight = swiglu_backward(
        gathered[:, :hidden], gathered[:, hidden : 2 * hidden], gathered[:, 2 * hidden :], rows_p
    )
    part_x = rows_x
    part_dy = rows_dy
    weighted = stacked[:, :hidden]
    grad_gate_pre = stacked[:, hidden : 2 * hidden]
    grad_up_pre = stacked[:, 2 * hidden :]
    grad_gate = contract_first(part_x, grad_gate_pre)
    grad_up = contract_first(part_x, grad_up_pre)
    grad_down = contract_first(weighted, part_dy)
    row_grads = contract_last(grad_gate_pre, w_gate) + contract_last(grad_up_pre, w_up)
    route_dx = row_grads.astype(jnp.bfloat16)
    route_dp = grad_weight
    result = (grad_gate, grad_up, grad_down, route_dx, route_dp)
    grad_gate, grad_up, grad_down, route_dx, route_dp = result
    back_dx, back_dp = (
        lax.all_to_all(
            route_dx.reshape(experts, capacity, features),
            "expert",
            split_axis=0,
            concat_axis=0,
            tiled=True,
        ),
        lax.all_to_all(
            route_dp.reshape(experts, capacity), "expert", split_axis=0, concat_axis=0, tiled=True
        ),
    )
    picked_dx = back_dx.reshape(total_rows, features)[position]
    picked_dp = back_dp.reshape(total_rows)[position]
    grad_tokens = jnp.sum(
        picked_dx.reshape(tok_dev, per_token, features).astype(jnp.float32), axis=1
    ).astype(jnp.bfloat16)
    grad_probs = picked_dp.reshape(tok_dev, per_token)
    return (grad_tokens, grad_probs, grad_gate[None], grad_up[None], grad_down[None])


def solution(mesh):
    return jax.shard_map(
        per_device,
        mesh=mesh,
        in_specs=(
            P("expert", "dp"),
            P("expert", "dp"),
            P("expert", None),
            P("expert", None),
            P("expert", "dp", None),
            P("expert", "dp", None),
            P("expert", None, "dp"),
        ),
        out_specs=(
            P("expert", "dp"),
            P("expert", None),
            P("expert", "dp", None),
            P("expert", "dp", None),
            P("expert", None, "dp"),
        ),
        check_vma=False,
    )
```

profile of v0, /device:TPU:1, one launch (start us, length us, event | category | flops | bytes accessed | tf_op | source)
XLA Modules:
  0.0 505.9 jit_solution(6566596041197735945)
XLA Ops:
  7.2 0.8 copy.19
  8.2 0.7 broadcast_multiply_fusion
  10.0 1.9 scatter_custom_fusion.1
  11.9 20.4 %all-to-all-start.1 = ((bf16[32,16,128]{2,1,0:T(8,128)(2,1)}), bf16[32,16,128]{2,1,0:T(8,128)(2,1)S(1)}, u32[]{:S(2)}, u32[]{:S(2)}) async-start(bf16[32,16,128]{2,1,0:T(8,128)(2,1)} %bitcast.4), calls=%async_computation.1 | async-start | bytes 262144 | tf_op jit(solution)/shard_map/all_to_all | solution.py:59
  32.3 1.9 scatter_custom_fusion.2
  34.3 13.9 %all-to-all-done.1 = bf16[32,16,128]{2,1,0:T(8,128)(2,1)S(1)} async-done(((bf16[32,16,128]{2,1,0:T(8,128)(2,1)}), bf16[32,16,128]{2,1,0:T(8,128)(2,1)S(1)}, u32[]{:S(2)}, u32[]{:S(2)}) %all-to-all-start.1) | async-done | bytes 131104 | tf_op jit(solution)/shard_map/all_to_all | solution.py:59
  48.2 5.8 %all-to-all-start.2 = ((bf16[32,16,128]{2,1,0:T(8,128)(2,1)}), bf16[32,16,128]{2,1,0:T(8,128)(2,1)}, u32[]{:S(2)}, u32[]{:S(2)}) async-start(bf16[32,16,128]{2,1,0:T(8,128)(2,1)} %bitcast.9), calls=%async_computation.2 | async-start | bytes 262144 | tf_op jit(solution)/shard_map/all_to_all | solution.py:66
  54.1 1.5 fusion.10
  55.6 2.2 fusion.6
  57.8 12.4 %all-to-all-done.2 = bf16[32,16,128]{2,1,0:T(8,128)(2,1)} async-done(((bf16[32,16,128]{2,1,0:T(8,128)(2,1)}), bf16[32,16,128]{2,1,0:T(8,128)(2,1)}, u32[]{:S(2)}, u32[]{:S(2)}) %all-to-all-start.2) | async-done | bytes 131104 | tf_op jit(solution)/shard_map/all_to_all | solution.py:66
  70.2 3.3 fusion.3
  73.5 7.2 %pad_maximum_fusion = f32[512,4608]{1,0:T(8,128)} fusion(f32[512,1536]{1,0:T(8,128)} %fusion.3, f32[512,1536]{1,0:T(8,128)} %fusion.6, f32[512,1536]{1,0:T(8,128)S(1)} %fusion.10), kind=kLoop, calls=%fused_computation.5 | loop fusion | flops 4718592 | bytes 18874368 | tf_op jit(solution)/shard_map/concatenate | solution.py:86
  80.7 235.2 %reduce-scatter.2.cloned.1.call-done = f32[16,4608]{1,0:T(8,128)} async-done(((f32[512,4608]{1,0:T(8,128)}), f32[16,4608]{1,0:T(8,128)}) %reduce-scatter.2.cloned.1.call-update) | async-done | bytes 294928 | tf_op jit(solution)/shard_map/reduce_scatter | solution.py:85
  316.1 2.2 scatter_custom_fusion
  318.3 0.7 all_to_all.25
  319.0 17.8 %all-to-all-start = ((bf16[32,1,16]{2,1,0:T(2,128)(2,1)}), bf16[32,1,16]{2,1,0:T(2,128)(2,1)S(1)}, u32[]{:S(2)}, u32[]{:S(2)}) async-start(bf16[32,1,16]{2,1,0:T(2,128)(2,1)} %all_to_all.25), calls=%async_computation | async-start | bytes 32768 | tf_op jit(solution)/shard_map/all_to_all | solution.py:73
  336.9 11.7 %all-to-all-done = bf16[32,1,16]{2,1,0:T(2,128)(2,1)S(1)} async-done(((bf16[32,1,16]{2,1,0:T(2,128)(2,1)}), bf16[32,1,16]{2,1,0:T(2,128)(2,1)S(1)}, u32[]{:S(2)}, u32[]{:S(2)}) %all-to-all-start) | async-done | bytes 1056 | tf_op jit(solution)/shard_map/all_to_all | solution.py:73
  348.7 93.5 %all-gather.2.cloned.1.call-done = f32[512,4608]{1,0:T(8,128)} async-done(((f32[16,4608]{1,0:T(8,128)}), f32[512,4608]{1,0:T(8,128)}) %all-gather.2.cloned.1.call-update) | async-done | bytes 9437200 | tf_op jit(solution)/shard_map/all_gather | solution.py:91
  442.2 5.1 multiply_convert_fusion.1
  447.9 1.3 convolution_bitcast_fusion.1
  449.2 1.2 fusion.2
  450.4 0.7 convert_element_type.56
  451.1 14.1 %all-to-all-start.4 = ((bf16[32,1,16]{2,1,0:T(2,128)(2,1)}), bf16[32,1,16]{2,1,0:T(2,128)(2,1)S(1)}, u32[]{:S(2)}, u32[]{:S(2)}) async-start(bf16[32,1,16]{2,1,0:T(2,128)(2,1)} %convert_element_type.56), calls=%async_computation.5 | async-start | bytes 32768 | tf_op jit(solution)/shard_map/all_to_all | solution.py:116
  465.3 1.3 convolution_bitcast_fusion.2
  466.6 10.4 %all-to-all-done.4 = bf16[32,1,16]{2,1,0:T(2,128)(2,1)S(1)} async-done(((bf16[32,1,16]{2,1,0:T(2,128)(2,1)}), bf16[32,1,16]{2,1,0:T(2,128)(2,1)S(1)}, u32[]{:S(2)}, u32[]{:S(2)}) %all-to-all-start.4) | async-done | bytes 1056 | tf_op jit(solution)/shard_map/all_to_all | solution.py:116
  477.0 4.4 all-to-all-start.3
  481.4 4.8 convolution_bitcast_fusion
  486.4 1.9 gather_fusion.1
  488.4 0.7 copy.25
  489.1 8.5 %all-to-all-done.3 = bf16[32,16,128]{2,1,0:T(8,128)(2,1)S(1)} async-done(((bf16[32,16,128]{2,1,0:T(8,128)(2,1)}), bf16[32,16,128]{2,1,0:T(8,128)(2,1)S(1)}, u32[]{:S(2)}, u32[]{:S(2)}) %all-to-all-start.3) | async-done | bytes 131104 | tf_op jit(solution)/shard_map/all_to_all | solution.py:109
  497.6 0.9 gather_fusion
  498.5 0.6 bitcast_reduce_fusion
  (38 shorter events, 2.5 us)
Async XLA Ops:
  7.2 46.9 %copy-start = (bf16[1,128,1536]{2,1,0:T(8,128)(2,1)S(1)}, bf16[1,128,1536]{2,1,0:T(8,128)(2,1)}, u32[]{:S(2)}) copy-start(bf16[1,128,1536]{2,1,0:T(8,128)(2,1)} %param.11) | copy-start | bytes 1179652
  11.9 36.3 %all-to-all-start.1 = ((bf16[32,16,128]{2,1,0:T(8,128)(2,1)}), bf16[32,16,128]{2,1,0:T(8,128)(2,1)S(1)}, u32[]{:S(2)}, u32[]{:S(2)}) async-start(bf16[32,16,128]{2,1,0:T(8,128)(2,1)} %bitcast.4), calls=%async_computation.1 | async-start | bytes 262144 | tf_op jit(solution)/shard_map/all_to_all | solution.py:59
  48.2 5.8 %copy-start.1 = (bf16[32,16,128]{2,1,0:T(8,128)(2,1)}, bf16[32,16,128]{2,1,0:T(8,128)(2,1)S(1)}, u32[]{:S(2)}) copy-start(bf16[32,16,128]{2,1,0:T(8,128)(2,1)S(1)} %all-to-all-done.1) | copy-start | bytes 393220
  48.2 22.0 %all-to-all-start.2 = ((bf16[32,16,128]{2,1,0:T(8,128)(2,1)}), bf16[32,16,128]{2,1,0:T(8,128)(2,1)}, u32[]{:S(2)}, u32[]{:S(2)}) async-start(bf16[32,16,128]{2,1,0:T(8,128)(2,1)} %bitcast.9), calls=%async_computation.2 | async-start | bytes 262144 | tf_op jit(solution)/shard_map/all_to_all | solution.py:66
  54.0 262.0 %reduce-scatter.2.cloned.1.call-start = ((), (), s32[]{:S(2)}) async-start(), calls=%async_computation.6 | async-start | bytes 9732096 | tf_op jit(solution)/shard_map/reduce_scatter | solution.py:85
  54.0 1.6 copy-start.4
  54.0 1.5 copy-start.2
  80.6 235.3 %copy-start.6 = (bf16[32,8]{0,1:T(8,128)(2,1)S(1)}, bf16[32,8]{0,1:T(8,128)(2,1)}, u32[]{:S(2)}) copy-start(bf16[32,8]{0,1:T(8,128)(2,1)} %param.10) | copy-start | bytes 1540
  80.7 361.6 %all-gather.2.cloned.1.call-start = ((), (), s32[]{:S(2)}) async-start(), calls=%async_computation.7 | async-start | bytes 9732096 | tf_op jit(solution)/shard_map/all_gather | solution.py:91
  319.0 29.6 %all-to-all-start = ((bf16[32,1,16]{2,1,0:T(2,128)(2,1)}), bf16[32,1,16]{2,1,0:T(2,128)(2,1)S(1)}, u32[]{:S(2)}, u32[]{:S(2)}) async-start(bf16[32,1,16]{2,1,0:T(2,128)(2,1)} %all_to_all.25), calls=%async_computation | async-start | bytes 32768 | tf_op jit(solution)/shard_map/all_to_all | solution.py:73
  348.7 99.2 %copy-start.3 = (bf16[32,16,128]{2,1,0:T(8,128)(2,1)S(1)}, bf16[32,16,128]{2,1,0:T(8,128)(2,1)}, u32[]{:S(2)}) copy-start(bf16[32,16,128]{2,1,0:T(8,128)(2,1)} %copy-done.1) | copy-start | bytes 393220
  447.3 1.9 copy-start.5
  451.1 25.9 %all-to-all-start.4 = ((bf16[32,1,16]{2,1,0:T(2,128)(2,1)}), bf16[32,1,16]{2,1,0:T(2,128)(2,1)S(1)}, u32[]{:S(2)}, u32[]{:S(2)}) async-start(bf16[32,1,16]{2,1,0:T(2,128)(2,1)} %convert_element_type.56), calls=%async_computation.5 | async-start | bytes 32768 | tf_op jit(solution)/shard_map/all_to_all | solution.py:116
  477.0 20.6 %all-to-all-start.3 = ((bf16[32,16,128]{2,1,0:T(8,128)(2,1)}), bf16[32,16,128]{2,1,0:T(8,128)(2,1)S(1)}, u32[]{:S(2)}, u32[]{:S(2)}) async-start(bf16[32,16,128]{2,1,0:T(8,128)(2,1)} %bitcast.12), calls=%async_computation.4 | async-start | bytes 262144 | tf_op jit(solution)/shard_map/all_to_all | solution.py:109
Sparse Core Ops, SparseCore 0:
  80.8 235.1 reduce-scatter.1
  320.2 121.9 all-gather.1
where the time goes:
time: 507 us; the launch traced here: 506 us
  waiting for transfers between devices  386 us (76%)
  starting transfers between devices  62.7 us (12%)
  matrix products  16.2 us (3%)
  other arithmetic  14.4 us (3%)
  between operations  14.2 us (3%)
  local copies, waits for them, and re-layouts  12.7 us (3%)
    reduce_scatter x1, waiting for transfers between devices, per_device(): lax.psum_scatter(jnp.concatenate((gate_part, up_part, back_part), axis=1)...  235 us
    all_gather x1, waiting for transfers between devices, per_device(): gathered = lax.all_gather(summed, 'dp', axis=0, tiled=True)  93.5 us
    all_to_all x1, starting transfers between devices, per_device(): lax.all_to_all(send_x.reshape(experts, capacity, features), 'expert', spl...  20.4 us
    all_to_all x1, starting transfers between devices, per_device(): lax.all_to_all(send_p.reshape(experts, capacity), 'expert', split_axis=0,...  17.8 us
    all_to_all x1, starting transfers between devices, per_device(): lax.all_to_all(route_dp.reshape(experts, capacity), 'expert', split_axis=...  14.1 us
    all_to_all x1, waiting for transfers between devices, per_device(): lax.all_to_all(send_x.reshape(experts, capacity, features), 'expert', spl...  13.9 us
    all_to_all x1, waiting for transfers between devices, per_device(): lax.all_to_all(send_dy.reshape(experts, capacity, features), 'expert', sp...  12.4 us
    all_to_all x1, waiting for transfers between devices, per_device(): lax.all_to_all(send_p.reshape(experts, capacity), 'expert', split_axis=0,...  11.7 us
  transfers between devices with their start and end apart: 7, of which 7 were waited for; matrix products, arithmetic and copies ran while one was open for 3% of the time, Pallas kernels for 0%

commit v1 on v0

v1 whole, which is shorter than its diff:
```python
import functools

import jax
import jax.numpy as jnp
from jax import lax
from jax.experimental import pallas as pl
from jax.experimental.pallas import tpu as pltpu
from jax.sharding import PartitionSpec as P

MESH = pl.DeviceIdType.MESH
F32, BF16 = jnp.float32, jnp.bfloat16
RING_X = 4
RS_SPLIT = (1024, 512)
AG_SPLIT = (896, 640)


def nt(a, b):
    return lax.dot_general(a, b, (((1,), (1,)), ((), ())), preferred_element_type=F32)


def nn(a, b):
    return jnp.dot(a, b, preferred_element_type=F32)


def iota(shape, dim):
    return lax.broadcasted_iota(jnp.int32, shape, dim)


def pieces(width, step=256):
    return [(c, min(step, width - c)) for c in range(0, width, step)]


class Ring:
    def __init__(self, at, size, turn):
        self.at, self.size, self.turn = at, size, turn
        half = size // 2
        self.reach = {"f": half, "n": size - 1 - half}
        self.away = [("f", t) for t in range(1, half + 1)]
        self.away += [("n", t) for t in range(1, size - half)]

    def shift(self, hops):
        return lax.rem(self.at + self.turn * hops + 2 * self.size, self.size)

    def target(self, offset):
        if offset is None:
            return self.at
        side, t = offset
        return self.shift(-t if side == "f" else t)

    def origin(self, offset):
        if offset is None:
            return self.at
        side, t = offset
        return self.shift(t if side == "f" else -t)

    def following(self, side):
        return self.shift(-1 if side == "f" else 1)


def dist(offset):
    return 0 if offset is None else offset[1]


def kernel(ring_x, ring_y, cap, rs_split, ag_split, tokens, grad_out, ids, probs, w_gate, w_up, w_down,
           o_tokens, o_probs, o_gate, o_up, o_down,
           hot, hot_t, send_rows, rows, x_t, dy_t, prob_send, prob_recv, partial,
           a1_send, a1_recv, a2_send, a2_recv, b1_send, b1_recv, b2_send, b2_recv,
           gathered, dx_send, back, dp_send, dp_recv, spread,
           disp_s, disp_r, prob_s, prob_r, a1_s, a1_r, a2_s, a2_r, b1_s, b1_r, b2_s, b2_r,
           ga_s, ga_r, gb_s, gb_r, ret_s, ret_r, dp_s, dp_r, bc_s, bc_r):
    me, mine = lax.axis_index("expert"), lax.axis_index("dp")
    experts, group = lax.axis_size("expert"), ring_x * ring_y
    tok, features = tokens.shape
    top, hidden = ids.shape[1], w_gate.shape[1]
    slots = experts * cap
    turn = 1 - 2 * lax.rem(me, 2)
    rx = Ring(mine // ring_y, ring_x, turn)
    ry = Ring(lax.rem(mine, ring_y), ring_y, turn)
    ring_a, ring_b = (rx, ry), (ry, rx)

    def block_at(first, second, rings):
        bx, by = (first, second) if rings[0] is rx else (second, first)
        return bx * ring_y + by

    def neighbour(ring, side):
        to = ring.following(side)
        return {"dp": to * ring_y + ry.at} if ring is rx else {"dp": rx.at * ring_y + to}

    barrier = pltpu.get_barrier_semaphore()

    def greet(where):
        pl.semaphore_signal(barrier, inc=1, device_id=where, device_id_type=MESH)

    for r in range(1, experts):
        greet({"expert": lax.rem(me + r, experts)})
    greeted = experts - 1
    for ring in (rx, ry):
        for side in ("f", "n"):
            if ring.reach[side]:
                greet(neighbour(ring, side))
                greeted += 1
    on_diagonal = me == mine

    @pl.when(jnp.logical_not(on_diagonal))
    def _():
        greet({"dp": me})

    ids_b = ids[...].astype(F32).astype(BF16)
    eye = (iota((top, top), 0) == iota((top, top), 1)).astype(F32).astype(BF16)
    ids_t = nt(eye, ids_b)
    probs_t = nt(eye, probs[...])
    expert_row = iota((experts, tok), 0).astype(F32)
    chosen = jnp.zeros((experts, tok), F32)
    weight = jnp.zeros((experts, tok), F32)
    for k in range(top):
        hit = ids_t[k:k + 1, :] == expert_row
        chosen = chosen + jnp.where(hit, 1.0, 0.0)
        weight = weight + jnp.where(hit, probs_t[k:k + 1, :], 0.0)
    earlier = jnp.where(iota((tok, tok), 0) < iota((tok, tok), 1), 1.0, 0.0).astype(BF16)
    rank = jnp.where(chosen > 0.5, nn(chosen.astype(BF16), earlier), 128.0).astype(BF16)
    owner = jnp.where(iota((slots, experts), 0) // cap == iota((slots, experts), 1), 1.0, 0.0).astype(BF16)
    owner_t = jnp.where(iota((experts, slots), 1) // cap == iota((experts, slots), 0), 1.0, 0.0).astype(BF16)
    slot_col = lax.rem(iota((slots, tok), 0), cap).astype(F32)
    slot_row = lax.rem(iota((tok, slots), 1), cap).astype(F32)
    one_hot = jnp.where(nn(owner, rank) == slot_col, 1.0, 0.0)
    hot[...] = one_hot.astype(BF16)
    eye_t = jnp.where(iota((tok, tok), 0) == iota((tok, tok), 1), 1.0, 0.0).astype(BF16)
    rank_t = nt(eye_t, rank)
    hot_t[...] = jnp.where(nn(rank_t.astype(BF16), owner_t) == slot_row, 1.0, 0.0).astype(BF16)
    send_rows[:, :, 0:features] = nn(hot[...], tokens[...]).astype(BF16).reshape(experts, cap, features)
    send_rows[:, :, features:2 * features] = nn(hot[...], grad_out[...]).astype(BF16).reshape(experts, cap, features)
    slot_weight = jnp.sum(one_hot * nn(owner, weight.astype(BF16)), axis=1, keepdims=True)
    lane_slot = iota((slots, 128), 1) == lax.rem(iota((slots, 128), 0), cap)
    weight_rows = nn(owner_t, jnp.where(lane_slot, slot_weight, 0.0).astype(BF16))
    for e in range(experts):
        prob_send[e] = weight_rows[e:e + 1, :]
    rows[me] = send_rows[me]

    @pl.when(on_diagonal)
    def _():
        prob_recv[...] = prob_send[me]
        pl.semaphore_wait(barrier, greeted + group - 1)

    @pl.when(jnp.logical_not(on_diagonal))
    def _():
        pl.semaphore_wait(barrier, greeted)

    dispatch = []
    for r in range(1, experts):
        to = lax.rem(me + r, experts)
        copy = pltpu.make_async_remote_copy(
            send_rows.at[to], rows.at[me], disp_s.at[r], disp_r.at[r], {"expert": to}, MESH)
        copy.start()
        dispatch.append(copy)

    def prob_copy(r):
        to = lax.rem(me + r, experts)
        return pltpu.make_async_remote_copy(
            prob_send.at[to], prob_recv, prob_s.at[r], prob_r, {"expert": to}, MESH)

    @pl.when(on_diagonal)
    def _():
        for r in range(1, experts):
            prob_copy(r).start()

    for r in range(1, experts):
        dispatch[r - 1].wait_recv()

    rs_a, rs_b = rs_split
    width_a, width_b = 3 * rs_a, 3 * rs_b
    half = group // 2
    for part in range(2):
        blk = slice(part * half, (part + 1) * half)
        x = rows[blk, :, 0:features].reshape(half * cap, features)
        dy = rows[blk, :, features:2 * features].reshape(half * cap, features)
        for at, width, base in ((0, rs_a, 0), (rs_a, rs_b, width_a)):
            for c, n in pieces(width):
                for j, value in enumerate((
                    nn(x, w_gate[:, at + c:at + c + n]),
                    nn(x, w_up[:, at + c:at + c + n]),
                    nt(dy, w_down[at + c:at + c + n, :]),
                )):
                    col = base + j * width + c
                    partial[blk, :, col:col + n] = value.reshape(half, cap, n)

    plans = []
    for rings, base, width, bufs in (
        (ring_a, 0, width_a, (a1_send, a1_recv, a1_s, a1_r, a2_send, a2_recv, a2_s, a2_r)),
        (ring_b, width_a, width_b, (b1_send, b1_recv, b1_s, b1_r, b2_send, b2_recv, b2_s, b2_r)),
    ):
        first, second = rings
        inner = [None] + second.away
        one = {(o1, o2): i for i, (o1, o2) in enumerate((o1, o2) for o1 in first.away for o2 in inner)}
        two = {o2: i for i, o2 in enumerate(second.away)}
        plans.append((rings, base, width, bufs, one, two))

    def one_copy(plan, key):
        rings, _, _, bufs, one, _ = plan
        i = one[key]
        return pltpu.make_async_remote_copy(
            bufs[0].at[i], bufs[1].at[i], bufs[2].at[i], bufs[3].at[i], neighbour(rings[0], key[0][0]), MESH)

    def two_copy(plan, key):
        rings, _, _, bufs, _, two = plan
        i = two[key]
        return pltpu.make_async_remote_copy(
            bufs[4].at[i], bufs[5].at[i], bufs[6].at[i], bufs[7].at[i], neighbour(rings[1], key[0]), MESH)

    def arrived_one(plan, key, total):
        one_copy(plan, key).wait_recv()
        return total + plan[3][1][plan[4][key]].astype(F32)

    def arrived_two(plan, key, total):
        two_copy(plan, key).wait_recv()
        return total + plan[3][5][plan[5][key]]

    def own(plan, o1, o2):
        rings, base, width = plan[:3]
        return partial[block_at(rings[0].target(o1), rings[1].target(o2), rings), :, base:base + width]

    def reduced_first(plan, o2):
        total = own(plan, None, o2)
        for side in ("f", "n"):
            if plan[0][0].reach[side]:
                total = arrived_one(plan, ((side, 1), o2), total)
        return total

    furthest = ring_x // 2 + ring_y // 2
    for steps in range(furthest, 0, -1):
        for plan in plans:
            first, second = plan[0]
            for o1 in [None] + first.away:
                for o2 in [None] + second.away:
                    if dist(o1) + dist(o2) != steps:
                        continue
                    if o1 is not None:
                        side, t = o1
                        total = own(plan, o1, o2)
                        if t < first.reach[side]:
                            total = arrived_one(plan, ((side, t + 1), o2), total)
                        plan[3][0][plan[4][(o1, o2)]] = total.astype(BF16)
                        one_copy(plan, (o1, o2)).start()
                    else:
                        side, t = o2
                        total = reduced_first(plan, o2)
                        if t < second.reach[side]:
                            total = arrived_two(plan, (side, t + 1), total)
                        plan[3][4][plan[5][o2]] = total
                        two_copy(plan, o2).start()
    done = []
    for plan in plans:
        total = reduced_first(plan, None)
        for side in ("f", "n"):
            if plan[0][1].reach[side]:
                total = arrived_two(plan, (side, 1), total)
        done.append(total)

    @pl.when(jnp.logical_not(on_diagonal))
    def _():
        prob_copy(1).wait_recv()

    diagonal = iota((cap, 128), 0) == iota((cap, 128), 1)
    weight_col = jnp.sum(jnp.where(diagonal, prob_recv[...], 0.0), axis=1, keepdims=True)
    ag_a, ag_b = ag_split
    full_a = 3 * ag_a
    grad_weight = jnp.zeros((cap, 1), F32)
    for total, at, width in ((done[0], 0, rs_a), (done[1], rs_a, rs_b)):
        gate, up, bk = (total[:, j * width:(j + 1) * width] for j in range(3))
        sig = jax.nn.sigmoid(gate)
        active = gate * sig
        product = active * up
        grad_weight = grad_weight + jnp.sum(bk * product, axis=1, keepdims=True)
        scaled = weight_col * bk
        results = (
            (weight_col * product).astype(BF16),
            (scaled * up * sig * (1.0 + gate * (1.0 - sig))).astype(BF16),
            (scaled * active).astype(BF16),
        )
        for j, value in enumerate(results):
            for lo, hi, start, n in ((0, ag_a, 0, ag_a), (ag_a, ag_a + ag_b, full_a, ag_b)):
                a, b = max(lo, at), min(hi, at + width)
                if a < b:
                    col = start + j * n + a - lo
                    gathered[mine, :, col:col + b - a] = value[:, a - at:b - at]

    gathers = []
    for rings, base, width, sems in (
        (ring_b, 0, full_a, (ga_s, ga_r)), (ring_a, full_a, 3 * ag_b, (gb_s, gb_r))):
        first, second = rings
        keys = [("1", o1) for o1 in first.away]
        keys += [("2", o1, o2) for o1 in [None] + first.away for o2 in second.away]
        gathers.append((rings, base, width, sems, {k: i for i, k in enumerate(keys)}))

    def gather_copy(plan, key):
        rings, base, width, sems, index = plan
        if key[0] == "1":
            side, t = key[1]
            before = (side, t - 1) if t > 1 else None
            blk = block_at(rings[0].origin(before), rings[1].at, rings)
            to = neighbour(rings[0], side)
        else:
            side, t = key[2]
            before = (side, t - 1) if t > 1 else None
            blk = block_at(rings[0].origin(key[1]), rings[1].origin(before), rings)
            to = neighbour(rings[1], side)
        ref = gathered.at[blk, :, base:base + width]
        i = index[key]
        return pltpu.make_async_remote_copy(ref, ref, sems[0].at[i], sems[1].at[i], to, MESH)

    def gather_wait(plan, key):
        rings, base, width, sems, index = plan
        if key[0] == "1":
            blk = block_at(rings[0].origin(key[1]), rings[1].at, rings)
            to = neighbour(rings[0], key[1][0])
        else:
            blk = block_at(rings[0].origin(key[1]), rings[1].origin(key[2]), rings)
            to = neighbour(rings[1], key[2][0])
        ref = gathered.at[blk, :, base:base + width]
        i = index[key]
        pltpu.make_async_remote_copy(ref, ref, sems[0].at[i], sems[1].at[i], to, MESH).wait_recv()

    def onward(plan, o1):
        for side in ("f", "n"):
            if plan[0][1].reach[side]:
                gather_copy(plan, ("2", o1, (side, 1))).start()

    def gather_step(steps):
        for plan in gathers:
            first, second = plan[0]
            for o1 in [None] + first.away:
                for o2 in [None] + second.away:
                    if dist(o1) + dist(o2) != steps:
                        continue
                    if o2 is None:
                        side, t = o1
                        gather_wait(plan, ("1", o1))
                        if t < first.reach[side]:
                            gather_copy(plan, ("1", (side, t + 1))).start()
                        onward(plan, o1)
                    else:
                        side, t = o2
                        gather_wait(plan, ("2", o1, o2))
                        if t < second.reach[side]:
                            gather_copy(plan, ("2", o1, (side, t + 1))).start()

    for plan in gathers:
        for side in ("f", "n"):
            if plan[0][0].reach[side]:
                gather_copy(plan, ("1", (side, 1))).start()
        onward(plan, None)

    rounded = grad_weight.astype(BF16).astype(F32)
    dp_send[...] = jnp.sum(jnp.where(diagonal, rounded, 0.0), axis=0, keepdims=True)

    def dp_copy(slot, where):
        return pltpu.make_async_remote_copy(
            dp_send, dp_recv.at[slot], dp_s, dp_r.at[slot], {"expert": where}, MESH)

    @pl.when(jnp.logical_not(on_diagonal))
    def _():
        dp_copy(me, mine).start()

    for r in range(1, experts):
        dispatch[r - 1].wait_send()
    for rows_of in range(group // 8):
        x = rows[rows_of * 8:rows_of * 8 + 8]
        x_t[:, rows_of * 8 * cap:(rows_of + 1) * 8 * cap] = (
            x[:, :, 0:features].reshape(8 * cap, features).astype(F32).T.astype(BF16))
        dy_t[:, rows_of * 8 * cap:(rows_of + 1) * 8 * cap] = (
            x[:, :, features:2 * features].reshape(8 * cap, features).astype(F32).T.astype(BF16))
    gather_step(1)
    gather_step(2)

    def spread_copy(r):
        return pltpu.make_async_remote_copy(
            spread, spread, bc_s.at[r], bc_r, {"dp": lax.rem(me + r, group)}, MESH)

    @pl.when(on_diagonal)
    def _():
        for r in range(1, experts):
            prob_copy(r).wait_send()
            dp_copy(lax.rem(me + r, experts), lax.rem(me + r, experts)).wait_recv()
        dp_recv[me] = dp_send[...]
        values = dp_recv[...].reshape(experts, 128).astype(BF16)
        lane = iota((tok, 128), 1)
        result = jnp.zeros((tok, 128), F32)
        for k in range(top):
            pick = jnp.where(ids[:, k:k + 1] == iota((tok, experts), 1), 1.0, 0.0)
            row = nn(pick.astype(BF16), values)
            place = jnp.sum(jnp.where(pick > 0.5, rank_t, 0.0), axis=1, keepdims=True)
            found = jnp.sum(jnp.where(lane.astype(F32) == place, row, 0.0), axis=1, keepdims=True)
            result = jnp.where(lane == k, found, result)
        spread[...] = result.astype(BF16)
        for r in range(1, group):
            spread_copy(r).start()

    for steps in range(3, furthest + 1):
        gather_step(steps)

    def piece(blk, j, part):
        at, n = ((0, ag_a), (full_a, ag_b))[part]
        return gathered[blk, :, at + j * n:at + (j + 1) * n]

    for first in range(0, group, 8):
        blk = slice(first, first + 8)
        total = jnp.zeros((8 * cap, features), F32)
        for part, (at, n) in enumerate(((0, ag_a), (ag_a, ag_b))):
            total = total + nt(piece(blk, 1, part).reshape(8 * cap, n), w_gate[:, at:at + n])
            total = total + nt(piece(blk, 2, part).reshape(8 * cap, n), w_up[:, at:at + n])
        dx_send[blk] = total.astype(BF16).reshape(8, cap, features)
    returns = []
    for r in range(1, experts):
        to = lax.rem(me + r, experts)
        copy = pltpu.make_async_remote_copy(
            dx_send.at[to], back.at[me], ret_s.at[r], ret_r.at[r], {"expert": to}, MESH)
        copy.start()
        returns.append(copy)
    back[me] = dx_send[me]

    for part, (at, n) in enumerate(((0, ag_a), (ag_a, ag_b))):
        for c, m in pieces(n):
            start = (0, full_a)[part] + c
            for j, (left, out) in enumerate(((dy_t, o_down), (x_t, o_gate), (x_t, o_up))):
                right = gathered[:, :, start + j * n:start + j * n + m].reshape(slots, m)
                value = nn(left[...], right)
                if j == 0:
                    out[at + c:at + c + m, :] = value.T
                else:
                    out[:, at + c:at + c + m] = value

    @pl.when(jnp.logical_not(on_diagonal))
    def _():
        spread_copy(1).wait_recv()
        dp_copy(me, mine).wait_send()

    @pl.when(on_diagonal)
    def _():
        for r in range(1, group):
            spread_copy(r).wait_send()

    o_probs[...] = spread[:, 0:top]
    for plan in plans:
        for key in plan[4]:
            one_copy(plan, key).wait_send()
        for key in plan[5]:
            two_copy(plan, key).wait_send()
    for plan in gathers:
        for key in plan[4]:
            gather_copy(plan, key).wait_send()
    for copy in returns:
        copy.wait_recv()
    o_tokens[...] = nn(hot_t[...], back[...].reshape(slots, features)).astype(BF16)
    for copy in returns:
        copy.wait_send()


def per_device(tokens, grad_out, expert_ids, probs, gate_weight, up_weight, down_weight):
    tok, features = tokens.shape
    top = expert_ids.shape[1]
    hidden = gate_weight.shape[2]
    experts, group = lax.axis_size("expert"), lax.axis_size("dp")
    cap = min(tok, 2 * tok * top // experts)
    ring_x, ring_y = RING_X, group // RING_X
    slots = experts * cap
    wide_a, wide_b = 3 * RS_SPLIT[0], 3 * RS_SPLIT[1]
    n_a1, n_a2 = (ring_x - 1) * ring_y, ring_y - 1
    n_b1, n_b2 = (ring_y - 1) * ring_x, ring_x - 1
    vmem = pltpu.VMEM
    dma = pltpu.SemaphoreType.DMA
    buffers = [
        vmem((slots, tok), BF16), vmem((tok, slots), BF16),
        vmem((experts, cap, 2 * features), BF16), vmem((experts, cap, 2 * features), BF16),
        vmem((features, slots), BF16), vmem((features, slots), BF16),
        vmem((experts, 1, 128), F32), vmem((1, 128), F32),
        vmem((group, cap, 3 * hidden), F32),
        vmem((n_a1, cap, wide_a), BF16), vmem((n_a1, cap, wide_a), BF16),
        vmem((n_a2, cap, wide_a), F32), vmem((n_a2, cap, wide_a), F32),
        vmem((n_b1, cap, wide_b), BF16), vmem((n_b1, cap, wide_b), BF16),
        vmem((n_b2, cap, wide_b), F32), vmem((n_b2, cap, wide_b), F32),
        vmem((group, cap, 3 * hidden), BF16),
        vmem((experts, cap, features), BF16), vmem((experts, cap, features), BF16),
        vmem((1, 128), F32), vmem((experts, 1, 128), F32), vmem((tok, 128), BF16),
    ]
    sems = [
        dma((experts,)), dma((experts,)), dma((experts,)), dma(()),
        dma((n_a1,)), dma((n_a1,)), dma((n_a2,)), dma((n_a2,)),
        dma((n_b1,)), dma((n_b1,)), dma((n_b2,)), dma((n_b2,)),
        dma((n_b2 * ring_y + n_a2,)), dma((n_b2 * ring_y + n_a2,)),
        dma((n_a2 * ring_x + n_b2,)), dma((n_a2 * ring_x + n_b2,)),
        dma((experts,)), dma((experts,)), dma(()), dma((experts,)), dma((group,)), dma(()),
    ]
    flops = 2 * slots * features * hidden * 8
    out = pl.pallas_call(
        functools.partial(kernel, ring_x, ring_y, cap, RS_SPLIT, AG_SPLIT),
        out_shape=(
            jax.ShapeDtypeStruct((tok, features), BF16),
            jax.ShapeDtypeStruct((tok, top), BF16),
            jax.ShapeDtypeStruct((features, hidden), F32),
            jax.ShapeDtypeStruct((features, hidden), F32),
            jax.ShapeDtypeStruct((hidden, features), F32),
        ),
        in_specs=[pl.BlockSpec(memory_space=pltpu.VMEM)] * 7,
        out_specs=[pl.BlockSpec(memory_space=pltpu.VMEM)] * 5,
        scratch_shapes=buffers + sems,
        compiler_params=pltpu.CompilerParams(
            collective_id=0, has_side_effects=True, vmem_limit_bytes=58 * 1024 * 1024),
        cost_estimate=pl.CostEstimate(flops=flops, bytes_accessed=4 * 1024 * 1024, transcendentals=0),
    )(tokens, grad_out, expert_ids, probs, gate_weight[0], up_weight[0], down_weight[0])
    grad_tokens, grad_probs, grad_gate, grad_up, grad_down = out
    return grad_tokens, grad_probs, grad_gate[None], grad_up[None], grad_down[None]


def solution(mesh):
    return jax.shard_map(
        per_device,
        mesh=mesh,
        in_specs=(
            P("expert", "dp"),
            P("expert", "dp"),
            P("expert", None),
            P("expert", None),
            P("expert", "dp", None),
            P("expert", "dp", None),
            P("expert", None, "dp"),
        ),
        out_specs=(
            P("expert", "dp"),
            P("expert", None),
            P("expert", "dp", None),
            P("expert", "dp", None),
            P("expert", None, "dp"),
        ),
        check_vma=False,
    )
```

time: 507 us -> 138 us (0.27)
  waiting for transfers between devices: 386 us -> 0 us
  Pallas kernels: 0 us -> 128 us
  starting transfers between devices: 62.7 us -> 0 us
  matrix products: 16.2 us -> 0 us
  other arithmetic: 14.4 us -> 0 us
  between operations: 14.2 us -> 0.67 us
    reduce_scatter x1 -> x0, waiting for transfers between devices: 235 us -> none  [per_device(): lax.psum_scatter(jnp.concatenate((gate_part, up_part, back_part), axis=1)...]
    pallas_call x0 -> x1, Pallas kernels: none -> 128 us  [per_device(): pl.pallas_call(functools.partial(kernel, ring_x, ring_y, cap, RS_SPLIT, A...]
    all_gather x1 -> x0, waiting for transfers between devices: 93.5 us -> none  [per_device(): gathered = lax.all_gather(summed, 'dp', axis=0, tiled=True)]
    all_to_all x5 -> x0, starting transfers between devices: 62.6 us -> none  [the longest x1 20.4 us: per_device(): lax.all_to_all(send_x.reshape(experts, capacity, features), 'expert', spl...]
    all_to_all x5 -> x0, waiting for transfers between devices: 56.9 us -> none  [the longest x1 13.9 us: per_device(): lax.all_to_all(send_x.reshape(experts, capacity, features), 'expert', spl...]
    dot_general x8 -> x0, matrix products: 16.2 us -> none  [the longest x3 7.41 us: contract_first(): lax.dot_general(left_side, right_side, (((0,), (0,)), ((), ())), preferre...]
    concatenate x1 -> x0, other arithmetic: 7.16 us -> none  [per_device(): jnp.concatenate((gate_part, up_part, back_part), axis=1)]
    unnamed x17 -> x19, local copies, waits for them, and re-layouts: 1.61 us -> 8.42 us
  transfers between devices with their start and end apart: 7 -> 0, of which waited for: 7 -> 0; matrix products, arithmetic and copies ran while one was open for 3% -> 0% of each run, Pallas kernels for 0% -> 0%
where the time goes in v1:
time: 138 us; the launch traced here: 137 us
  Pallas kernels  128 us (93%)
  local copies, waits for them, and re-layouts  8.42 us (6%)
    pallas_call x1, Pallas kernels, per_device(): pl.pallas_call(functools.partial(kernel, ring_x, ring_y, cap, RS_SPLIT, A...  128 us
    unnamed x19, local copies, waits for them, and re-layouts  8.42 us

profile of v1, /device:TPU:1, one launch (start us, length us, event | category | flops | bytes accessed | tf_op | source)
XLA Modules:
  0.0 137.4 jit_solution(14795087548932368260)
XLA Ops:
  0.6 0.0 copy-start.5
  0.6 0.7 copy-done.5
  1.3 0.0 copy-start.4
  1.3 0.7 copy.13.probs
  2.0 0.0 copy-done.4
  2.0 0.7 copy.12.ids
  2.7 128.3 %shard_map.110 = (bf16[32,128]{1,0:T(8,128)(2,1)}, bf16[32,8]{1,0:T(8,128)(2,1)}, f32[128,1536]{1,0:T(8,128)}, f32[128,1536]{1,0:T(8,128)}, f32[1536,128]{1,0:T(8,128)}) custom-call(bf16[32,128]{1,0:T(8,128)(2,1)} %tokens.1, bf16[32,128]{1,0:T(8,128)(2,1)} %grad_out.1, s32[32,8]{1,0:T(8,128)} %copy.12.ids, bf16[32,8]{1,0:T(8,128)(2,1)} %copy.13.probs, ...), custom_call_target="tpu_custom_call" | custom-call | flops 1610612736 | bytes 4194304 | tf_op jit(solution)/shard_map/pallas_call | solution.py:493
  131.0 0.0 copy-start.2
  131.0 0.0 copy-start.3
  131.0 0.7 copy-done.2
  131.7 0.7 copy.14
  132.4 0.0 copy-done.3
  132.4 0.6 copy.19
  133.0 0.0 copy-start.1
  133.0 2.1 %copy.20 = f32[1,128,1536]{2,1,0:T(8,128)} copy(f32[1,128,1536]{2,1,0:T(8,128)} %bitcast.8) | data formatting | bytes 1572864
  135.1 0.0 copy-done.1
  135.1 0.0 copy-start
  135.1 0.9 copy.21
  136.0 0.5 copy-done
  136.5 0.9 copy.22
Async XLA Ops:
  0.6 0.7 copy-start.5
  1.3 0.7 copy-start.4
  131.0 0.7 copy-start.2
  131.0 1.3 copy-start.3
  133.0 2.1 %copy-start.1 = (f32[128,1536]{1,0:T(8,128)S(1)}, f32[128,1536]{1,0:T(8,128)}, u32[]{:S(2)}) copy-start(f32[128,1536]{1,0:T(8,128)} %get-tuple-element.13) | copy-start | bytes 2359300
  135.1 1.4 %copy-start = (f32[1536,128]{1,0:T(8,128)S(1)}, f32[1536,128]{1,0:T(8,128)}, u32[]{:S(2)}) copy-start(f32[1536,128]{1,0:T(8,128)} %get-tuple-element.14) | copy-start | bytes 2359300

commit v2 on v1

--- a/solution.py
+++ b/solution.py
@@ -12,6 +12,8 @@
 RING_X = 4
 RS_SPLIT = (1024, 512)
 AG_SPLIT = (896, 640)
+SENDS = (3, 4)
+CUTS = 2
 
 
 def nt(a, b):
@@ -61,17 +63,18 @@
     return 0 if offset is None else offset[1]
 
 
-def kernel(ring_x, ring_y, cap, rs_split, ag_split, tokens, grad_out, ids, probs, w_gate, w_up, w_down,
+def kernel(ring_x, ring_y, cap, rs_split, ag_split, tokens, grad_out, ids, probs, h_gate, h_up, h_down,
            o_tokens, o_probs, o_gate, o_up, o_down,
+           w_gate, w_up, w_down, g_gate, g_up, g_down,
            hot, hot_t, send_rows, rows, x_t, dy_t, prob_send, prob_recv, partial,
            a1_send, a1_recv, a2_send, a2_recv, b1_send, b1_recv, b2_send, b2_recv,
            gathered, dx_send, back, dp_send, dp_recv, spread,
-           disp_s, disp_r, prob_s, prob_r, a1_s, a1_r, a2_s, a2_r, b1_s, b1_r, b2_s, b2_r,
+           load_s, store_s, disp_s, disp_r, prob_s, prob_r, a1_s, a1_r, a2_s, a2_r, b1_s, b1_r, b2_s, b2_r,
            ga_s, ga_r, gb_s, gb_r, ret_s, ret_r, dp_s, dp_r, bc_s, bc_r):
     me, mine = lax.axis_index("expert"), lax.axis_index("dp")
     experts, group = lax.axis_size("expert"), ring_x * ring_y
     tok, features = tokens.shape
-    top, hidden = ids.shape[1], w_gate.shape[1]
+    top = ids.shape[0]
     slots = experts * cap
     turn = 1 - 2 * lax.rem(me, 2)
     rx = Ring(mine // ring_y, ring_x, turn)
@@ -105,10 +108,15 @@
     def _():
         greet({"dp": me})
 
-    ids_b = ids[...].astype(F32).astype(BF16)
-    eye = (iota((top, top), 0) == iota((top, top), 1)).astype(F32).astype(BF16)
-    ids_t = nt(eye, ids_b)
-    probs_t = nt(eye, probs[...])
+    loads = [
+        pltpu.make_async_copy(src, dst, load_s.at[i])
+        for i, (src, dst) in enumerate(((h_gate, w_gate), (h_up, w_up), (h_down, w_down)))
+    ]
+    for copy in loads:
+        copy.start()
+
+    ids_t = ids[...].astype(F32)
+    probs_t = probs[...].astype(F32)
     expert_row = iota((experts, tok), 0).astype(F32)
     chosen = jnp.zeros((experts, tok), F32)
     weight = jnp.zeros((experts, tok), F32)
@@ -145,34 +153,68 @@
     def _():
         pl.semaphore_wait(barrier, greeted)
 
-    dispatch = []
-    for r in range(1, experts):
+    offsets = [(ox, oy) for ox in [None] + rx.away for oy in [None] + ry.away]
+    offsets.sort(key=lambda o: -dist(o[0]) - dist(o[1]))
+    place = {o: i for i, o in enumerate(offsets)}
+    furthest = ring_x // 2 + ring_y // 2
+    levels = (max(furthest - 2, 1), max(furthest - 3, 1), 0)
+    waves = []
+    for w, level in enumerate(levels):
+        above = levels[w - 1] if w else furthest + 1
+        waves.append([o for o in offsets if level <= dist(o[0]) + dist(o[1]) < above])
+
+    def target(o):
+        return rx.target(o[0]) * ring_y + ry.target(o[1])
+
+    def arrived(o):
+        source = target(o)
+
+        @pl.when(source != me)
+        def _():
+            pltpu.make_async_remote_copy(
+                send_rows.at[0], rows.at[source], disp_s.at[0], disp_r.at[source], {"expert": source}, MESH,
+            ).wait_recv()
+
+    def dispatch_copy(r):
         to = lax.rem(me + r, experts)
-        copy = pltpu.make_async_remote_copy(
-            send_rows.at[to], rows.at[me], disp_s.at[r], disp_r.at[r], {"expert": to}, MESH)
-        copy.start()
-        dispatch.append(copy)
+        return pltpu.make_async_remote_copy(
+            send_rows.at[to], rows.at[me], disp_s.at[r], disp_r.at[me], {"expert": to}, MESH)
+
+    apart_x = lax.rem(me // ring_y - rx.at + ring_x, ring_x)
+    apart_y = lax.rem(lax.rem(me, ring_y) - ry.at + ring_y, ring_y)
+    apart = jnp.minimum(apart_x, ring_x - apart_x) + jnp.minimum(apart_y, ring_y - apart_y)
 
     def prob_copy(r):
         to = lax.rem(me + r, experts)
         return pltpu.make_async_remote_copy(
             prob_send.at[to], prob_recv, prob_s.at[r], prob_r, {"expert": to}, MESH)
 
+    @pl.when(apart >= levels[0])
+    def _():
+        for r in range(1, experts):
+            dispatch_copy(r).start()
+
+    for o in waves[0]:
+        arrived(o)
+
+    @pl.when(apart < levels[0])
+    def _():
+        for r in range(1, experts):
+            dispatch_copy(r).start()
+
     @pl.when(on_diagonal)
     def _():
         for r in range(1, experts):
             prob_copy(r).start()
 
-    for r in range(1, experts):
-        dispatch[r - 1].wait_recv()
-
     rs_a, rs_b = rs_split
     width_a, width_b = 3 * rs_a, 3 * rs_b
-    half = group // 2
-    for part in range(2):
-        blk = slice(part * half, (part + 1) * half)
-        x = rows[blk, :, 0:features].reshape(half * cap, features)
-        dy = rows[blk, :, features:2 * features].reshape(half * cap, features)
+
+    def multiply(wave):
+        lo, count = place[wave[0]], len(wave)
+        blk = slice(lo, lo + count)
+        block = jnp.concatenate([rows[target(o)] for o in wave], axis=0)
+        x, dy = block[:, 0:features], block[:, features:2 * features]
         for at, width, base in ((0, rs_a, 0), (rs_a, rs_b, width_a)):
             for c, n in pieces(width):
                 for j, value in enumerate((
@@ -181,7 +223,11 @@
                     nt(dy, w_down[at + c:at + c + n, :]),
                 )):
                     col = base + j * width + c
-                    partial[blk, :, col:col + n] = value.reshape(half, cap, n)
+                    partial[blk, :, col:col + n] = value.reshape(count, cap, n)
+
+    for copy in loads:
+        copy.wait()
+    multiply(waves[0])
 
     plans = []
     for rings, base, width, bufs in (
@@ -216,7 +262,7 @@
 
     def own(plan, o1, o2):
         rings, base, width = plan[:3]
-        return partial[block_at(rings[0].target(o1), rings[1].target(o2), rings), :, base:base + width]
+        return partial[place[(o1, o2) if rings[0] is rx else (o2, o1)], :, base:base + width]
 
     def reduced_first(plan, o2):
         total = own(plan, None, o2)
@@ -225,8 +271,14 @@
                 total = arrived_one(plan, ((side, 1), o2), total)
         return total
 
-    furthest = ring_x // 2 + ring_y // 2
-    for steps in range(furthest, 0, -1):
+    for steps in range(furthest, -1, -1):
+        for w in (1, 2):
+            if waves[w] and steps == max(dist(o[0]) + dist(o[1]) for o in waves[w]):
+                for o in waves[w]:
+                    arrived(o)
+                multiply(waves[w])
+        if not steps:
+            break
         for plan in plans:
             first, second = plan[0]
             for o1 in [None] + first.away:
@@ -247,13 +299,13 @@
                             total = arrived_two(plan, (side, t + 1), total)
                         plan[3][4][plan[5][o2]] = total
                         two_copy(plan, o2).start()
-    done = []
-    for plan in plans:
+
+    def reduced(plan):
         total = reduced_first(plan, None)
         for side in ("f", "n"):
             if plan[0][1].reach[side]:
                 total = arrived_two(plan, (side, 1), total)
-        done.append(total)
+        return total
 
     @pl.when(jnp.logical_not(on_diagonal))
     def _():
@@ -263,26 +315,6 @@
     weight_col = jnp.sum(jnp.where(diagonal, prob_recv[...], 0.0), axis=1, keepdims=True)
     ag_a, ag_b = ag_split
     full_a = 3 * ag_a
-    grad_weight = jnp.zeros((cap, 1), F32)
-    for total, at, width in ((done[0], 0, rs_a), (done[1], rs_a, rs_b)):
-        gate, up, bk = (total[:, j * width:(j + 1) * width] for j in range(3))
-        sig = jax.nn.sigmoid(gate)
-        active = gate * sig
-        product = active * up
-        grad_weight = grad_weight + jnp.sum(bk * product, axis=1, keepdims=True)
-        scaled = weight_col * bk
-        results = (
-            (weight_col * product).astype(BF16),
-            (scaled * up * sig * (1.0 + gate * (1.0 - sig))).astype(BF16),
-            (scaled * active).astype(BF16),
-        )
-        for j, value in enumerate(results):
-            for lo, hi, start, n in ((0, ag_a, 0, ag_a), (ag_a, ag_a + ag_b, full_a, ag_b)):
-                a, b = max(lo, at), min(hi, at + width)
-                if a < b:
-                    col = start + j * n + a - lo
-                    gathered[mine, :, col:col + b - a] = value[:, a - at:b - at]
-
     gathers = []
     for rings, base, width, sems in (
         (ring_b, 0, full_a, (ga_s, ga_r)), (ring_a, full_a, 3 * ag_b, (gb_s, gb_r))):
@@ -343,12 +375,36 @@
                         if t < second.reach[side]:
                             gather_copy(plan, ("2", o1, (side, t + 1))).start()
 
-    for plan in gathers:
+    def begin(plan):
         for side in ("f", "n"):
             if plan[0][0].reach[side]:
                 gather_copy(plan, ("1", (side, 1))).start()
         onward(plan, None)
 
+    grad_weight = jnp.zeros((cap, 1), F32)
+    for which, at, width in ((0, 0, rs_a), (1, rs_a, rs_b)):
+        total = reduced(plans[which])
+        gate, up, bk = (total[:, j * width:(j + 1) * width] for j in range(3))
+        sig = jax.nn.sigmoid(gate)
+        active = gate * sig
+        product = active * up
+        grad_weight = grad_weight + jnp.sum(bk * product, axis=1, keepdims=True)
+        scaled = weight_col * bk
+        results = (
+            (weight_col * product).astype(BF16),
+            (scaled * up * sig * (1.0 + gate * (1.0 - sig))).astype(BF16),
+            (scaled * active).astype(BF16),
+        )
+        for j, value in enumerate(results):
+            for lo, hi, start, n in ((0, ag_a, 0, ag_a), (ag_a, ag_a + ag_b, full_a, ag_b)):
+                a, b = max(lo, at), min(hi, at + width)
+                if a < b:
+                    col = start + j * n + a - lo
+                    gathered[mine, :, col:col + b - a] = value[:, a - at:b - at]
+        for part, n in ((0, ag_a), (1, ag_a + ag_b)):
+            if at < n <= at + width:
+                begin(gathers[part])
+
     rounded = grad_weight.astype(BF16).astype(F32)
     dp_send[...] = jnp.sum(jnp.where(diagonal, rounded, 0.0), axis=0, keepdims=True)
 
@@ -361,7 +417,7 @@
         dp_copy(me, mine).start()
 
     for r in range(1, experts):
-        dispatch[r - 1].wait_send()
+        dispatch_copy(r).wait_send()
     for rows_of in range(group // 8):
         x = rows[rows_of * 8:rows_of * 8 + 8]
         x_t[:, rows_of * 8 * cap:(rows_of + 1) * 8 * cap] = (
@@ -383,50 +439,72 @@
         dp_recv[me] = dp_send[...]
         values = dp_recv[...].reshape(experts, 128).astype(BF16)
         lane = iota((tok, 128), 1)
+        ids_col = nt(eye_t, ids_t.astype(BF16))
         result = jnp.zeros((tok, 128), F32)
         for k in range(top):
-            pick = jnp.where(ids[:, k:k + 1] == iota((tok, experts), 1), 1.0, 0.0)
+            pick = jnp.where(ids_col[:, k:k + 1] == iota((tok, experts), 1).astype(F32), 1.0, 0.0)
             row = nn(pick.astype(BF16), values)
             place = jnp.sum(jnp.where(pick > 0.5, rank_t, 0.0), axis=1, keepdims=True)
             found = jnp.sum(jnp.where(lane.astype(F32) == place, row, 0.0), axis=1, keepdims=True)
             result = jnp.where(lane == k, found, result)
-        spread[...] = result.astype(BF16)
+        eye = jnp.where(iota((16, 128), 0) == iota((16, 128), 1), 1.0, 0.0).astype(BF16)
+        spread[...] = jnp.zeros_like(spread)
+        spread[:, 0:tok] = nt(eye, result.astype(BF16)).astype(BF16)
         for r in range(1, group):
             spread_copy(r).start()
 
+    def source(o):
+        return rx.origin(o[0]) * ring_y + ry.origin(o[1])
+
+    def return_copy(i, to):
+        return pltpu.make_async_remote_copy(
+            dx_send.at[i], back.at[me], ret_s.at[i], ret_r.at[me], {"expert": to}, MESH)
+
+    def send_home(low, high):
+        wave = [o for o in offsets if low <= dist(o[0]) + dist(o[1]) <= high]
+        lo, count = place[wave[0]], len(wave)
+        total = jnp.zeros((count * cap, features), F32)
+        for part, (at, n) in enumerate(((0, ag_a), (ag_a, ag_b))):
+            for j, w in ((1, w_gate), (2, w_up)):
+                begin_at = (0, full_a)[part] + j * n
+                left = jnp.concatenate([gathered[source(o), :, begin_at:begin_at + n] for o in wave], axis=0)
+                total = total + nt(left, w[:, at:at + n])
+        dx_send[lo:lo + count] = total.astype(BF16).reshape(count, cap, features)
+        for i in range(lo, lo + count):
+            to = source(offsets[i])
+
+            @pl.when(to != me)
+            def _():
+                return_copy(i, to).start()
+
+            @pl.when(to == me)
+            def _():
+                back[me] = dx_send[i]
+
+    bounds = SENDS
+    sent = -1
     for steps in range(3, furthest + 1):
         gather_step(steps)
-
-    def piece(blk, j, part):
-        at, n = ((0, ag_a), (full_a, ag_b))[part]
-        return gathered[blk, :, at + j * n:at + (j + 1) * n]
-
-    for first in range(0, group, 8):
-        blk = slice(first, first + 8)
-        total = jnp.zeros((8 * cap, features), F32)
-        for part, (at, n) in enumerate(((0, ag_a), (ag_a, ag_b))):
-            total = total + nt(piece(blk, 1, part).reshape(8 * cap, n), w_gate[:, at:at + n])
-            total = total + nt(piece(blk, 2, part).reshape(8 * cap, n), w_up[:, at:at + n])
-        dx_send[blk] = total.astype(BF16).reshape(8, cap, features)
-    returns = []
-    for r in range(1, experts):
-        to = lax.rem(me + r, experts)
-        copy = pltpu.make_async_remote_copy(
-            dx_send.at[to], back.at[me], ret_s.at[r], ret_r.at[r], {"expert": to}, MESH)
-        copy.start()
-        returns.append(copy)
-    back[me] = dx_send[me]
+        if steps in bounds or steps == furthest:
+            send_home(sent + 1, steps)
+            sent = steps
 
     for part, (at, n) in enumerate(((0, ag_a), (ag_a, ag_b))):
         for c, m in pieces(n):
             start = (0, full_a)[part] + c
-            for j, (left, out) in enumerate(((dy_t, o_down), (x_t, o_gate), (x_t, o_up))):
+            for j, (left, out) in enumerate(((dy_t, g_down), (x_t, g_gate), (x_t, g_up))):
                 right = gathered[:, :, start + j * n:start + j * n + m].reshape(slots, m)
                 value = nn(left[...], right)
                 if j == 0:
                     out[at + c:at + c + m, :] = value.T
                 else:
                     out[:, at + c:at + c + m] = value
+    stores = [
+        pltpu.make_async_copy(src, dst, store_s.at[i])
+        for i, (src, dst) in enumerate(((g_gate, o_gate), (g_up, o_up), (g_down, o_down)))
+    ]
+    for copy in stores:
+        copy.start()
 
     @pl.when(jnp.logical_not(on_diagonal))
     def _():
@@ -438,7 +516,7 @@
         for r in range(1, group):
             spread_copy(r).wait_send()
 
-    o_probs[...] = spread[:, 0:top]
+    o_probs[...] = spread[0:top, 0:tok]
     for plan in plans:
         for key in plan[4]:
             one_copy(plan, key).wait_send()
@@ -447,11 +525,38 @@
     for plan in gathers:
         for key in plan[4]:
             gather_copy(plan, key).wait_send()
-    for copy in returns:
-        copy.wait_recv()
+    for r in range(1, experts):
+        sender = lax.rem(me + r, experts)
+        pltpu.make_async_remote_copy(
+            dx_send.at[0], back.at[sender], ret_s.at[0], ret_r.at[sender], {"expert": sender}, MESH).wait_recv()
     o_tokens[...] = nn(hot_t[...], back[...].reshape(slots, features)).astype(BF16)
-    for copy in returns:
-        copy.wait_send()
+    for i, o in enumerate(offsets):
+        to = source(o)
+
+        @pl.when(to != me)
+        def _():
+            return_copy(i, to).wait_send()
+    for copy in stores:
+        copy.wait()
+
+
+def carry(parts, *refs):
+    ins, outs, held, in_s, out_s = refs[:5], refs[5:10], refs[10:15], refs[15], refs[16]
+    reads, writes = [], []
+    for src, dst, mid in zip(ins, outs, held):
+        rows = src.shape[0]
+        cuts = parts if rows > 32 else 1
+        for c in range(cuts):
+            at, i = slice(c * rows // cuts, (c + 1) * rows // cuts), len(reads)
+            reads.append(pltpu.make_async_copy(src.at[at], mid.at[at], in_s.at[i]))
+            writes.append(pltpu.make_async_copy(mid.at[at], dst.at[at], out_s.at[i]))
+    for copy in reads:
+        copy.start()
+    for read, write in zip(reads, writes):
+        read.wait()
+        write.start()
+    for copy in writes:
+        copy.wait()
 
 
 def per_device(tokens, grad_out, expert_ids, probs, gate_weight, up_weight, down_weight):
@@ -468,6 +573,8 @@
     vmem = pltpu.VMEM
     dma = pltpu.SemaphoreType.DMA
     buffers = [
+        vmem((features, hidden), BF16), vmem((features, hidden), BF16), vmem((hidden, features), BF16),
+        vmem((features, hidden), F32), vmem((features, hidden), F32), vmem((hidden, features), F32),
         vmem((slots, tok), BF16), vmem((tok, slots), BF16),
         vmem((experts, cap, 2 * features), BF16), vmem((experts, cap, 2 * features), BF16),
         vmem((features, slots), BF16), vmem((features, slots), BF16),
@@ -479,9 +586,10 @@
         vmem((n_b2, cap, wide_b), F32), vmem((n_b2, cap, wide_b), F32),
         vmem((group, cap, 3 * hidden), BF16),
         vmem((experts, cap, features), BF16), vmem((experts, cap, features), BF16),
-        vmem((1, 128), F32), vmem((experts, 1, 128), F32), vmem((tok, 128), BF16),
+        vmem((1, 128), F32), vmem((experts, 1, 128), F32), vmem((16, 128), BF16),
     ]
     sems = [
+        dma((3,)), dma((3,)),
         dma((experts,)), dma((experts,)), dma((experts,)), dma(()),
         dma((n_a1,)), dma((n_a1,)), dma((n_a2,)), dma((n_a2,)),
         dma((n_b1,)), dma((n_b1,)), dma((n_b2,)), dma((n_b2,)),
@@ -494,20 +602,29 @@
         functools.partial(kernel, ring_x, ring_y, cap, RS_SPLIT, AG_SPLIT),
         out_shape=(
             jax.ShapeDtypeStruct((tok, features), BF16),
-            jax.ShapeDtypeStruct((tok, top), BF16),
+            jax.ShapeDtypeStruct((top, tok), BF16),
             jax.ShapeDtypeStruct((features, hidden), F32),
             jax.ShapeDtypeStruct((features, hidden), F32),
             jax.ShapeDtypeStruct((hidden, features), F32),
         ),
-        in_specs=[pl.BlockSpec(memory_space=pltpu.VMEM)] * 7,
-        out_specs=[pl.BlockSpec(memory_space=pltpu.VMEM)] * 5,
+        in_specs=[pl.BlockSpec(memory_space=pltpu.VMEM)] * 4 + [pl.BlockSpec(memory_space=pl.ANY)] * 3,
+        out_specs=[pl.BlockSpec(memory_space=pltpu.VMEM)] * 2 + [pl.BlockSpec(memory_space=pl.ANY)] * 3,
         scratch_shapes=buffers + sems,
         compiler_params=pltpu.CompilerParams(
             collective_id=0, has_side_effects=True, vmem_limit_bytes=58 * 1024 * 1024),
         cost_estimate=pl.CostEstimate(flops=flops, bytes_accessed=4 * 1024 * 1024, transcendentals=0),
-    )(tokens, grad_out, expert_ids, probs, gate_weight[0], up_weight[0], down_weight[0])
+    )(tokens, grad_out, expert_ids.T, probs.T, gate_weight[0], up_weight[0], down_weight[0])
+    out = pl.pallas_call(
+        functools.partial(carry, CUTS),
+        out_shape=[jax.ShapeDtypeStruct(o.shape, o.dtype) for o in out],
+        in_specs=[pl.BlockSpec(memory_space=pl.ANY)] * 5,
+        out_specs=[pl.BlockSpec(memory_space=pl.ANY)] * 5,
+        scratch_shapes=[vmem(o.shape, o.dtype) for o in out] + [dma((2 + 3 * CUTS,))] * 2,
+        compiler_params=pltpu.CompilerParams(vmem_limit_bytes=58 * 1024 * 1024),
+        cost_estimate=pl.CostEstimate(flops=0, bytes_accessed=5 * 1024 * 1024, transcendentals=0),
+    )(*out)
     grad_tokens, grad_probs, grad_gate, grad_up, grad_down = out
-    return grad_tokens, grad_probs, grad_gate[None], grad_up[None], grad_down[None]
+    return grad_tokens, grad_probs.T, grad_gate[None], grad_up[None], grad_down[None]
 
 
 def solution(mesh):

time: 138 us -> 119 us (0.86)
  the two profiles are of different devices: /device:TPU:1 before, /device:TPU:130 now
where the time goes in v2:
time: 119 us
  Pallas kernels  118 us (99%)
    pallas_call x1, Pallas kernels, per_device(): pl.pallas_call(functools.partial(kernel, ring_x, ring_y, cap, RS_SPLIT, A...  115 us
    pallas_call x1, Pallas kernels, per_device(): pl.pallas_call(functools.partial(carry, CUTS), out_shape=[jax.ShapeDtypeS...  2.55 us

profile of v2, /device:TPU:130, one launch (start us, length us, event | category | flops | bytes accessed | tf_op | source)
XLA Modules:
  0.0 118.6 jit_solution(11753766684246880202)
XLA Ops:
  0.6 115.5 %shard_map.110 = (bf16[32,128]{1,0:T(8,128)(2,1)}, bf16[8,32]{1,0:T(8,128)(2,1)}, f32[128,1536]{1,0:T(8,128)}, f32[128,1536]{1,0:T(8,128)}, f32[1536,128]{1,0:T(8,128)}) custom-call(bf16[32,128]{1,0:T(8,128)(2,1)} %tokens.1, bf16[32,128]{1,0:T(8,128)(2,1)} %grad_out.1, s32[8,32]{1,0:T(8,128)} %bitcast.15, bf16[8,32]{1,0:T(8,128)(2,1)} %bitcast.16, ...), custom_call_target="tpu_custom_call" | custom-call | flops 1610612736 | bytes 4194304 | tf_op jit(solution)/shard_map/pallas_call | solution.py:601
  116.1 2.5 %shard_map.111 = (bf16[32,128]{1,0:T(8,128)(2,1)}, bf16[8,32]{1,0:T(8,128)(2,1)}, f32[128,1536]{1,0:T(8,128)}, f32[128,1536]{1,0:T(8,128)}, f32[1536,128]{1,0:T(8,128)}) custom-call(bf16[32,128]{1,0:T(8,128)(2,1)} %get-tuple-element.15.refs_0_, bf16[8,32]{1,0:T(8,128)(2,1)} %get-tuple-element.16.refs_1_, f32[128,1536]{1,0:T(8,128)} %get-tuple-element.17.refs_2_, ...), custom_call_target="tpu_custom_call" | custom-call | bytes 5242880 | tf_op jit(solution)/shard_map/pallas_call | solution.py:617

commit v3 on v2

--- a/solution.py
+++ b/solution.py
@@ -10,9 +10,9 @@
 MESH = pl.DeviceIdType.MESH
 F32, BF16 = jnp.float32, jnp.bfloat16
 RING_X = 4
-RS_SPLIT = (1024, 512)
+RS_SPLIT = (896, 640)
 AG_SPLIT = (896, 640)
-SENDS = (3, 4)
+SENDS = (3, 4, 5)
 CUTS = 2
 
 
@@ -67,7 +67,7 @@
            o_tokens, o_probs, o_gate, o_up, o_down,
            w_gate, w_up, w_down, g_gate, g_up, g_down,
            hot, hot_t, send_rows, rows, x_t, dy_t, prob_send, prob_recv, partial,
-           a1_send, a1_recv, a2_send, a2_recv, b1_send, b1_recv, b2_send, b2_recv,
+           a1_send, a1_recv, a2_send, a2_recv, a3_send, a3_recv, b1_send, b1_recv, b2_send, b2_recv,
            gathered, dx_send, back, dp_send, dp_recv, spread,
            load_s, store_s, disp_s, disp_r, prob_s, prob_r, a1_s, a1_r, a2_s, a2_r, b1_s, b1_r, b2_s, b2_r,
            ga_s, ga_r, gb_s, gb_r, ret_s, ret_r, dp_s, dp_r, bc_s, bc_r):
@@ -231,7 +231,7 @@
 
     plans = []
     for rings, base, width, bufs in (
-        (ring_a, 0, width_a, (a1_send, a1_recv, a1_s, a1_r, a2_send, a2_recv, a2_s, a2_r)),
+        (ring_a, 0, width_a, (a1_send, a1_recv, a1_s, a1_r, a2_send, a2_recv, a2_s, a2_r, a3_send, a3_recv)),
         (ring_b, width_a, width_b, (b1_send, b1_recv, b1_s, b1_r, b2_send, b2_recv, b2_s, b2_r)),
     ):
         first, second = rings
@@ -246,11 +246,17 @@
         return pltpu.make_async_remote_copy(
             bufs[0].at[i], bufs[1].at[i], bufs[2].at[i], bufs[3].at[i], neighbour(rings[0], key[0][0]), MESH)
 
+    def sides(plan, key):
+        bufs = plan[3]
+        early = plan[0][1].reach[key[0]] - key[1] < 2
+        return bufs[8:10] if len(bufs) > 8 and early else bufs[4:6]
+
     def two_copy(plan, key):
         rings, _, _, bufs, _, two = plan
         i = two[key]
+        src, dst = sides(plan, key)
         return pltpu.make_async_remote_copy(
-            bufs[4].at[i], bufs[5].at[i], bufs[6].at[i], bufs[7].at[i], neighbour(rings[1], key[0]), MESH)
+            src.at[i], dst.at[i], bufs[6].at[i], bufs[7].at[i], neighbour(rings[1], key[0]), MESH)
 
     def arrived_one(plan, key, total):
         one_copy(plan, key).wait_recv()
@@ -258,7 +264,7 @@
 
     def arrived_two(plan, key, total):
         two_copy(plan, key).wait_recv()
-        return total + plan[3][5][plan[5][key]]
+        return total + sides(plan, key)[1][plan[5][key]].astype(F32)
 
     def own(plan, o1, o2):
         rings, base, width = plan[:3]
@@ -297,7 +303,8 @@
                         total = reduced_first(plan, o2)
                         if t < second.reach[side]:
                             total = arrived_two(plan, (side, t + 1), total)
-                        plan[3][4][plan[5][o2]] = total
+                        store = sides(plan, o2)[0]
+                        store[plan[5][o2]] = total.astype(store.dtype)
                         two_copy(plan, o2).start()
 
     def reduced(plan):
@@ -582,6 +589,7 @@
         vmem((group, cap, 3 * hidden), F32),
         vmem((n_a1, cap, wide_a), BF16), vmem((n_a1, cap, wide_a), BF16),
         vmem((n_a2, cap, wide_a), F32), vmem((n_a2, cap, wide_a), F32),
+        vmem((n_a2, cap, wide_a), BF16), vmem((n_a2, cap, wide_a), BF16),
         vmem((n_b1, cap, wide_b), BF16), vmem((n_b1, cap, wide_b), BF16),
         vmem((n_b2, cap, wide_b), F32), vmem((n_b2, cap, wide_b), F32),
         vmem((group, cap, 3 * hidden), BF16),

time: 119 us -> 115 us (0.966)
  the two profiles are of different devices: /device:TPU:130 before, /device:TPU:45 now
where the time goes in v3:
time: 115 us
  Pallas kernels  115 us (100%)
    pallas_call x1, Pallas kernels, per_device(): pl.pallas_call(functools.partial(kernel, ring_x, ring_y, cap, RS_SPLIT, A...  112 us
    pallas_call x1, Pallas kernels, per_device(): pl.pallas_call(functools.partial(carry, CUTS), out_shape=[jax.ShapeDtypeS...  2.55 us

profile of v3, /device:TPU:45, one launch (start us, length us, event | category | flops | bytes accessed | tf_op | source)
XLA Modules:
  0.0 115.2 jit_solution(6192953051816654843)
XLA Ops:
  0.6 112.0 %shard_map.110 = (bf16[32,128]{1,0:T(8,128)(2,1)}, bf16[8,32]{1,0:T(8,128)(2,1)}, f32[128,1536]{1,0:T(8,128)}, f32[128,1536]{1,0:T(8,128)}, f32[1536,128]{1,0:T(8,128)}) custom-call(bf16[32,128]{1,0:T(8,128)(2,1)} %tokens.1, bf16[32,128]{1,0:T(8,128)(2,1)} %grad_out.1, s32[8,32]{1,0:T(8,128)} %bitcast.15, bf16[8,32]{1,0:T(8,128)(2,1)} %bitcast.16, ...), custom_call_target="tpu_custom_call" | custom-call | flops 1610612736 | bytes 4194304 | tf_op jit(solution)/shard_map/pallas_call | solution.py:609
  112.7 2.5 %shard_map.111 = (bf16[32,128]{1,0:T(8,128)(2,1)}, bf16[8,32]{1,0:T(8,128)(2,1)}, f32[128,1536]{1,0:T(8,128)}, f32[128,1536]{1,0:T(8,128)}, f32[1536,128]{1,0:T(8,128)}) custom-call(bf16[32,128]{1,0:T(8,128)(2,1)} %get-tuple-element.15.refs_0_, bf16[8,32]{1,0:T(8,128)(2,1)} %get-tuple-element.16.refs_1_, f32[128,1536]{1,0:T(8,128)} %get-tuple-element.17.refs_2_, ...), custom_call_target="tpu_custom_call" | custom-call | bytes 5242880 | tf_op jit(solution)/shard_map/pallas_call | solution.py:625

commit v4 on v3

--- a/solution.py
+++ b/solution.py
@@ -363,7 +363,7 @@
             if plan[0][1].reach[side]:
                 gather_copy(plan, ("2", o1, (side, 1))).start()
 
-    def gather_step(steps):
+    def gather_step(steps, meanwhile=lambda count: None):
         for plan in gathers:
             first, second = plan[0]
             for o1 in [None] + first.away:
@@ -381,6 +381,7 @@
                         gather_wait(plan, ("2", o1, o2))
                         if t < second.reach[side]:
                             gather_copy(plan, ("2", o1, (side, t + 1))).start()
+                    meanwhile(3)
 
     def begin(plan):
         for side in ("f", "n"):
@@ -425,12 +426,35 @@
 
     for r in range(1, experts):
         dispatch_copy(r).wait_send()
-    for rows_of in range(group // 8):
-        x = rows[rows_of * 8:rows_of * 8 + 8]
-        x_t[:, rows_of * 8 * cap:(rows_of + 1) * 8 * cap] = (
-            x[:, :, 0:features].reshape(8 * cap, features).astype(F32).T.astype(BF16))
-        dy_t[:, rows_of * 8 * cap:(rows_of + 1) * 8 * cap] = (
-            x[:, :, features:2 * features].reshape(8 * cap, features).astype(F32).T.astype(BF16))
+    def source(o):
+        return rx.origin(o[0]) * ring_y + ry.origin(o[1])
+
+    homeward = sorted(offsets, key=lambda o: -dist(o[0]) - dist(o[1]))
+    late = 8 if group >= 16 else group // 2
+    for first in range(0, group, late):
+        block = jnp.concatenate([rows[source(o)] for o in homeward[first:first + late]], axis=0).astype(F32)
+        lanes = slice(first * cap, (first + late) * cap)
+        x_t[:, lanes] = block[:, 0:features].T.astype(BF16)
+        dy_t[:, lanes] = block[:, features:2 * features].T.astype(BF16)
+
+    def weight_chunk(part, c, m, j, first, last):
+        at, n = ((0, ag_a), (ag_a, ag_b))[part]
+        start = (0, full_a)[part] + c + j * n
+        left, out = ((dy_t, g_down), (x_t, g_gate), (x_t, g_up))[j]
+        right = jnp.concatenate([gathered[source(o), :, start:start + m] for o in homeward[first:last]], axis=0)
+        value = nn(left[:, first * cap:last * cap], right)
+        ref = out.at[at + c:at + c + m, :] if j == 0 else out.at[:, at + c:at + c + m]
+        value = value.T if j == 0 else value
+        ref[...] = value if first else ref[...] + value
+
+    chunks = [
+        (part, c, m, j) for part, n in enumerate((ag_a, ag_b)) for c, m in pieces(n) for j in range(3)]
+    todo = list(chunks)
+
+    def meanwhile(count):
+        for _ in range(min(count, len(todo))):
+            weight_chunk(*todo.pop(0), late, group)
+
     gather_step(1)
     gather_step(2)
 
@@ -460,16 +484,13 @@
         for r in range(1, group):
             spread_copy(r).start()
 
-    def source(o):
-        return rx.origin(o[0]) * ring_y + ry.origin(o[1])
-
     def return_copy(i, to):
         return pltpu.make_async_remote_copy(
             dx_send.at[i], back.at[me], ret_s.at[i], ret_r.at[me], {"expert": to}, MESH)
 
     def send_home(low, high):
-        wave = [o for o in offsets if low <= dist(o[0]) + dist(o[1]) <= high]
-        lo, count = place[wave[0]], len(wave)
+        wave = [o for o in homeward if low <= dist(o[0]) + dist(o[1]) <= high]
+        lo, count = homeward.index(wave[0]), len(wave)
         total = jnp.zeros((count * cap, features), F32)
         for part, (at, n) in enumerate(((0, ag_a), (ag_a, ag_b))):
             for j, w in ((1, w_gate), (2, w_up)):
@@ -478,7 +499,7 @@
                 total = total + nt(left, w[:, at:at + n])
         dx_send[lo:lo + count] = total.astype(BF16).reshape(count, cap, features)
         for i in range(lo, lo + count):
-            to = source(offsets[i])
+            to = source(homeward[i])
 
             @pl.when(to != me)
             def _():
@@ -491,21 +512,14 @@
     bounds = SENDS
     sent = -1
     for steps in range(3, furthest + 1):
-        gather_step(steps)
+        gather_step(steps, meanwhile if steps >= furthest - 1 else lambda count: None)
         if steps in bounds or steps == furthest:
             send_home(sent + 1, steps)
             sent = steps
 
-    for part, (at, n) in enumerate(((0, ag_a), (ag_a, ag_b))):
-        for c, m in pieces(n):
-            start = (0, full_a)[part] + c
-            for j, (left, out) in enumerate(((dy_t, g_down), (x_t, g_gate), (x_t, g_up))):
-                right = gathered[:, :, start + j * n:start + j * n + m].reshape(slots, m)
-                value = nn(left[...], right)
-                if j == 0:
-                    out[at + c:at + c + m, :] = value.T
-                else:
-                    out[:, at + c:at + c + m] = value
+    meanwhile(len(todo))
+    for chunk in chunks:
+        weight_chunk(*chunk, 0, late)
     stores = [
         pltpu.make_async_copy(src, dst, store_s.at[i])
         for i, (src, dst) in enumerate(((g_gate, o_gate), (g_up, o_up), (g_down, o_down)))
@@ -537,7 +551,7 @@
         pltpu.make_async_remote_copy(
             dx_send.at[0], back.at[sender], ret_s.at[0], ret_r.at[sender], {"expert": sender}, MESH).wait_recv()
     o_tokens[...] = nn(hot_t[...], back[...].reshape(slots, features)).astype(BF16)
-    for i, o in enumerate(offsets):
+    for i, o in enumerate(homeward):
         to = source(o)
 
         @pl.when(to != me)

time: 115 us -> 116 us (level)
  the two profiles are of different devices: /device:TPU:45 before, /device:TPU:125 now
where the time goes in v4:
time: 116 us
  Pallas kernels  115 us (99%)
    pallas_call x1, Pallas kernels, per_device(): pl.pallas_call(functools.partial(kernel, ring_x, ring_y, cap, RS_SPLIT, A...  113 us
    pallas_call x1, Pallas kernels, per_device(): pl.pallas_call(functools.partial(carry, CUTS), out_shape=[jax.ShapeDtypeS...  2.55 us

profile of v4, /device:TPU:125, one launch (start us, length us, event | category | flops | bytes accessed | tf_op | source)
XLA Modules:
  0.0 115.7 jit_solution(10485519436901226743)
XLA Ops:
  0.6 112.5 %shard_map.110 = (bf16[32,128]{1,0:T(8,128)(2,1)}, bf16[8,32]{1,0:T(8,128)(2,1)}, f32[128,1536]{1,0:T(8,128)}, f32[128,1536]{1,0:T(8,128)}, f32[1536,128]{1,0:T(8,128)}) custom-call(bf16[32,128]{1,0:T(8,128)(2,1)} %tokens.1, bf16[32,128]{1,0:T(8,128)(2,1)} %grad_out.1, s32[8,32]{1,0:T(8,128)} %bitcast.15, bf16[8,32]{1,0:T(8,128)(2,1)} %bitcast.16, ...), custom_call_target="tpu_custom_call" | custom-call | flops 1610612736 | bytes 4194304 | tf_op jit(solution)/shard_map/pallas_call | solution.py:623
  113.2 2.5 %shard_map.111 = (bf16[32,128]{1,0:T(8,128)(2,1)}, bf16[8,32]{1,0:T(8,128)(2,1)}, f32[128,1536]{1,0:T(8,128)}, f32[128,1536]{1,0:T(8,128)}, f32[1536,128]{1,0:T(8,128)}) custom-call(bf16[32,128]{1,0:T(8,128)(2,1)} %get-tuple-element.15.refs_0_, bf16[8,32]{1,0:T(8,128)(2,1)} %get-tuple-element.16.refs_1_, f32[128,1536]{1,0:T(8,128)} %get-tuple-element.17.refs_2_, ...), custom_call_target="tpu_custom_call" | custom-call | bytes 5242880 | tf_op jit(solution)/shard_map/pallas_call | solution.py:639
